TPU v7x, 32 devices: a whole 2x2x4 slice. The times are simulated.
32 devices in a mesh: row: 4 (over y, x), col: 8 (over z, core).
Axes of the slice: x: 2, y: 2, z: 4, core: 2. Of those that a mesh axis runs over, the one named last changes fastest.
Arguments:
- tokens: bfloat16 [2048, 1536], P('row', 'col'), may hold values from -6 to 6
- weight: bfloat16 [1536, 49152], P('row', 'col'), may hold values from -0.15625 to 0.15625
- counts: int32 [4], P('row'), may hold values from 1 to 512
- owner: int32 [4], replicated, may hold values from 0 to 3, each once
Outputs:
- window_product: float32 [2048, 49152], P('row', 'col')
Inputs may be any that keep to these rules, and one draw needn't show every extreme that they name: `owner`: each number occurs once.
All inputs are finite; a program needn't handle non-finite values.
Results may differ from a plain program's by a relative error of at most 0.0003.
Values may be sent and summed in bfloat16 or wider, within the bound.
A program may use at most 128 MiB of HBM per device.

v0:
```python
import jax
import jax.numpy as jnp
from jax import lax
from jax.sharding import PartitionSpec as P


def align_panels(gathered, owner):
    row_count = gathered.shape[0]
    panels = owner.shape[0]
    slotted = gathered.reshape(row_count, panels, gathered.shape[1] // panels)
    return jnp.take(slotted, owner, axis=1).reshape(row_count, gathered.shape[1])


def per_device(tokens, weight, counts, owner):
    row_count = tokens.shape[0]
    aligned = align_panels(lax.all_gather(tokens, "col", axis=1, tiled=True), owner)
    gathered_w = lax.all_gather(weight, "row", axis=0, tiled=True)
    product = jnp.dot(aligned, gathered_w, preferred_element_type=jnp.float32)
    token_limit = counts[0]
    kept = jnp.arange(row_count, dtype=jnp.int32) < token_limit
    return jnp.where(kept[:, None], product, jnp.float32(0.0))


def solution(mesh):
    in_specs = (P("row", "col"), P("row", "col"), P("row"), P())
    out_specs = P("row", "col")
    return jax.shard_map(
        per_device, mesh=mesh, in_specs=in_specs, out_specs=out_specs, check_vma=False
    )
```

profile of v0, /device:TPU:0, one launch (start us, length us, event | category | flops | bytes accessed | tf_op | source)
XLA Modules:
  0.0 237.8 jit_solution(8108246910956820529)
XLA Ops:
  6.5 0.0 all-gather.3.cloned.1.call-start
  6.5 0.7 all-gather.3.cloned.1.call-update
  7.3 0.0 copy-start
  7.3 0.0 all-gather.5.cloned.1.call-start
  7.3 0.7 all-gather.5.cloned.1.call-update
  8.7 0.0 copy-done
  8.7 0.1 broadcast_in_dim.30
  8.8 28.0 %all-gather.3.cloned.1.call-done = bf16[512,1536]{0,1:T(8,128)(2,1)} async-done(((bf16[512,192]{0,1:T(8,128)(2,1)}), bf16[512,1536]{0,1:T(8,128)(2,1)}) %all-gather.3.cloned.1.call-update) | async-done | bytes 1572880 | tf_op jit(solution)/shard_map/all_gather | solution.py:16
  36.8 2.1 gather_fusion
  38.8 0.3 bitcast_select_fusion
  39.2 175.0 %all-gather.5.cloned.1.call-done = bf16[1536,6144]{1,0:T(8,128)(2,1)} async-done(((bf16[384,6144]{1,0:T(8,128)(2,1)}), bf16[1536,6144]{1,0:T(8,128)(2,1)}) %all-gather.5.cloned.1.call-update) | async-done | bytes 18874384 | tf_op jit(solution)/shard_map/all_gather | solution.py:17
  214.2 16.8 %convolution_select_fusion = f32[512,6144]{1,0:T(8,128)} fusion(bf16[512,1536]{0,1:T(8,128)(2,1)S(1)} %bitcast_select_fusion, bf16[1536,6144]{1,0:T(8,128)(2,1)} %all-gather.5.cloned.1.call-done, pred[512]{0:T(512)(128)(4,1)S(1)} %iota_compare_fusion), kind=kOutput, calls=%fused_computation.1 | convolution fusion | flops 9666822144 | bytes 33030656 | tf_op jit(solution)/shard_map/dot_general | solution.py:18
  (5 shorter events, 0.0 us)
Async XLA Ops:
  6.5 30.2 %all-gather.3.cloned.1.call-start = ((), (), s32[]{:S(2)}) async-start(), calls=%async_computation | async-start | bytes 1769472 | tf_op jit(solution)/shard_map/all_gather | solution.py:16
  7.3 1.4 copy-start
  7.3 206.9 %all-gather.5.cloned.1.call-start = ((), (), s32[]{:S(2)}) async-start(), calls=%async_computation.1 | async-start | bytes 23592960 | tf_op jit(solution)/shard_map/all_gather | solution.py:17
Sparse Core Ops, SparseCore 0:
  9.0 27.7 all-gather.2
  38.6 175.4 all-gather.4
where the time goes:
time: 238 us
  waiting for transfers between devices  204 us (86%)
  matrix products  16.8 us (7%)
  between operations  14.1 us (6%)
    all_gather x1, waiting for transfers between devices, per_device(): gathered_w = lax.all_gather(weight, 'row', axis=0, tiled=True)  175 us
    all_gather x1, waiting for transfers between devices, per_device(): lax.all_gather(tokens, 'col', axis=1, tiled=True)  28 us
    dot_general x1, matrix products, per_device(): product = jnp.dot(aligned, gathered_w, preferred_element_type=jnp.float32)  16.8 us
  transfers between devices with their start and end apart: 2, of which 2 were waited for; matrix products, arithmetic and copies ran while one was open for 1% of the time, Pallas kernels for 0%

commit v1 on v0

v1 whole, which is shorter than its diff:
```python
import functools

import jax
import jax.numpy as jnp
from jax import lax
from jax.experimental import pallas as pl
from jax.experimental.pallas import tpu as pltpu
from jax.sharding import PartitionSpec as P

MESH = pl.DeviceIdType.MESH
GROUPS = 8


def align_panels(gathered, owner):
    row_count = gathered.shape[0]
    panels = owner.shape[0]
    slotted = gathered.reshape(row_count, panels, gathered.shape[1] // panels)
    return jnp.take(slotted, owner, axis=1).reshape(row_count, gathered.shape[1])


def per_device_general(tokens, weight, counts, owner):
    row_count = tokens.shape[0]
    aligned = align_panels(lax.all_gather(tokens, "col", axis=1, tiled=True), owner)
    gathered_w = lax.all_gather(weight, "row", axis=0, tiled=True)
    product = jnp.dot(aligned, gathered_w, preferred_element_type=jnp.float32)
    token_limit = counts[0]
    kept = jnp.arange(row_count, dtype=jnp.int32) < token_limit
    return jnp.where(kept[:, None], product, jnp.float32(0.0))


def kernel(
    orients, nc, cw,
    counts, owner, tok_in, w_in, out,
    tokb, al, wb, qb, qs, rb, rs, ob,
    tl_sem, ta_s, ta_r, tb_s, tb_r,
    wl_sem, px_s, px_r, py_s, py_r, fy_s, fy_r, ox_s, ox_r, os_s, os_r, ol_sem,
):
    rows, piece = tok_in.shape
    panel = w_in.shape[0]
    half = nc * cw
    row, col = lax.axis_index("row"), lax.axis_index("col")
    y, x = row // 2, row % 2
    z, core = col // 2, col % 2
    z_hi, z_lo = z // 2, z % 2
    x_dev = (y * 2 + (1 - x), col)
    y_dev = ((1 - y) * 2 + x, col)
    z1_dev = (row, (z_hi * 2 + (1 - z_lo)) * 2 + core)
    z2_dev = (row, ((1 - z_hi) * 2 + z_lo) * 2 + core)
    c_dev = (row, z * 2 + (1 - core))
    peers = (x_dev, y_dev, z1_dev, z2_dev, c_dev)

    barrier = pltpu.get_barrier_semaphore()
    for peer in peers:
        pl.semaphore_signal(barrier, inc=1, device_id=peer, device_id_type=MESH)
    pl.semaphore_wait(barrier, len(peers))

    def remote(src, dst, send, recv, dev):
        return pltpu.make_async_remote_copy(
            src_ref=src, dst_ref=dst, send_sem=send, recv_sem=recv,
            device_id=dev, device_id_type=MESH)

    a_dev = (x_dev, y_dev)
    b_dev = (y_dev, x_dev)
    side = (x, y)

    def cols(o, s, k):
        return pl.ds(pl.multiple_of(orients.index(o) * 2 * half + s * half + k * cw, 128), cw)

    def at(o, k):
        return orients.index(o) * nc + k

    def px(o, k):
        g = at(o, k)
        return remote(w_in.at[:, cols(o, 1 - side[o], k)], wb.at[g, 1 + o],
                      px_s.at[g], px_r.at[g], a_dev[o])

    def py(o, k):
        g = at(o, k)
        return remote(w_in.at[:, cols(o, side[o], k)], wb.at[g, 2 - o],
                      py_s.at[g], py_r.at[g], b_dev[o])

    def fy(o, k):
        g = at(o, k)
        return remote(wb.at[g, 1 + o], wb.at[g, 3], fy_s.at[g], fy_r.at[g], b_dev[o])

    def wl(o, k):
        g = at(o, k)
        return pltpu.make_async_copy(
            w_in.at[:, cols(o, side[o], k)], wb.at[g, 0], wl_sem.at[g])

    def ox(o, k):
        g = at(o, k)
        return remote(qb.at[g], rb.at[g], ox_s.at[g], ox_r.at[g], a_dev[o])

    def os_(o, k):
        g = at(o, k)
        return remote(qs.at[g], rs.at[g], os_s.at[g], os_r.at[g], a_dev[o])

    def out_own(o, k):
        g = at(o, k)
        return pltpu.make_async_copy(
            ob.at[0, g], out.at[:, cols(o, side[o], k)], ol_sem.at[0, g])

    def out_got(o, k):
        g = at(o, k)
        return pltpu.make_async_copy(
            ob.at[1, g], out.at[:, cols(o, 1 - side[o], k)], ol_sem.at[1, g])

    def each(f):
        def body(k, carry):
            for o in orients:
                f(o, k)
            return carry
        lax.fori_loop(0, nc, body, 0)

    own = pltpu.make_async_copy(tok_in, tokb.at[core, z, 0], tl_sem)
    own.start()
    first = [remote(tok_in, tokb.at[core, z, 1 + i], ta_s.at[i], ta_r.at[i], a_dev[o])
             for i, o in enumerate(orients)]
    for c in first:
        c.start()

    def start_weights(o, k):
        px(o, k).start()
        py(o, k).start()
        wl(o, k).start()
    each(start_weights)

    own.wait()
    for c in first:
        c.wait()
    pair = pl.ds(z_hi * 2, 2)
    steps = (
        remote(tokb.at[core, z], tokb.at[core, z], tb_s.at[0], tb_r.at[0], z1_dev),
        remote(tokb.at[core, pair], tokb.at[core, pair], tb_s.at[1], tb_r.at[1], z2_dev),
        remote(tokb.at[core], tokb.at[core], tb_s.at[2], tb_r.at[2], c_dev),
    )
    for c in steps:
        c.start()
        c.wait()

    order = (row, y * 2 + (1 - x), (1 - y) * 2 + x, (1 - y) * 2 + (1 - x))
    for j in range(4):
        slot = owner[order[j]]
        for s in range(1 + len(orients)):
            lo = tokb[0, slot, s]
            hi = tokb[1, slot, s]
            al[s, :, j * panel:(j + 1) * panel] = jnp.concatenate([lo, hi], axis=1)

    kept = lax.broadcasted_iota(jnp.int32, (rows, cw), 0) < counts[0]

    def forward(o, k):
        px(o, k).wait_recv()
        fy(o, k).start()

    ahead = 2
    for k in range(ahead):
        for o in orients:
            forward(o, k)

    def compute(o, k):
        g = at(o, k)

        @pl.when(k + ahead < nc)
        def _():
            forward(o, k + ahead)

        wl(o, k).wait()
        py(o, k).wait_recv()
        fy(o, k).wait_recv()
        w = wb[g].reshape(4 * panel, cw)
        theirs = jnp.dot(al[1 + orients.index(o)], w, preferred_element_type=jnp.float32)
        split = theirs.reshape(GROUPS, rows // GROUPS, cw)
        top = jnp.maximum(jnp.max(jnp.abs(split), axis=1), 1.2e-38)
        inverse = 1.0 / top
        levels = jnp.round((split * inverse[:, None, :]) * 32767.0)
        qb[g] = levels.astype(jnp.int32).astype(jnp.int16).reshape(rows, cw)
        qs[g] = top
        ox(o, k).start()
        os_(o, k).start()
        mine = jnp.dot(al[0], w, preferred_element_type=jnp.float32)
        ob[0, g] = jnp.where(kept, mine, 0.0)
        out_own(o, k).start()
    each(compute)

    def receive(o, k):
        g = at(o, k)
        ox(o, k).wait_recv()
        os_(o, k).wait_recv()
        levels = rb[g].astype(jnp.int32).astype(jnp.float32).reshape(GROUPS, rows // GROUPS, cw)
        value = levels * (rs[g] * (1.0 / 32767.0))[:, None, :]
        ob[1, g] = jnp.where(kept, value.reshape(rows, cw), 0.0)
        out_got(o, k).start()
    each(receive)

    def finish(o, k):
        for c in (px(o, k), py(o, k), fy(o, k), ox(o, k), os_(o, k)):
            c.wait_send()
        out_own(o, k).wait()
        out_got(o, k).wait()
    each(finish)


def per_device(tokens, weight, counts, owner):
    rows, piece = tokens.shape
    panel, width = weight.shape
    orients = (0, 1)
    cw = 256
    nc = width // (2 * len(orients) * cw)
    nct = nc * len(orients)
    sets = 1 + len(orients)
    dma = pltpu.SemaphoreType.DMA
    return pl.pallas_call(
        functools.partial(kernel, orients, nc, cw),
        out_shape=jax.ShapeDtypeStruct((rows, width), jnp.float32),
        in_specs=[pl.BlockSpec(memory_space=pltpu.SMEM)] * 2 + [pl.BlockSpec(memory_space=pl.ANY)] * 2,
        out_specs=pl.BlockSpec(memory_space=pl.ANY),
        scratch_shapes=[
            pltpu.VMEM((2, 4, sets, rows, piece), jnp.bfloat16),
            pltpu.VMEM((sets, rows, 4 * panel), jnp.bfloat16),
            pltpu.VMEM((nct, 4, panel, cw), jnp.bfloat16),
            pltpu.VMEM((nct, rows, cw), jnp.int16),
            pltpu.VMEM((nct, GROUPS, cw), jnp.float32),
            pltpu.VMEM((nct, rows, cw), jnp.int16),
            pltpu.VMEM((nct, GROUPS, cw), jnp.float32),
            pltpu.VMEM((2, nct, rows, cw), jnp.float32),
            dma, dma((len(orients),)), dma((len(orients),)), dma((3,)), dma((3,)),
        ] + [dma((nct,))] * 11 + [dma((2, nct))],
        compiler_params=pltpu.CompilerParams(
            collective_id=0, has_side_effects=True, vmem_limit_bytes=56 * 2**20),
        cost_estimate=pl.CostEstimate(
            flops=2 * rows * 4 * panel * width, bytes_accessed=8 * rows * width, transcendentals=0),
    )(counts, owner, tokens, weight)


def solution(mesh):
    in_specs = (P("row", "col"), P("row", "col"), P("row"), P())
    out_specs = P("row", "col")
    planned = dict(mesh.shape) == {"row": 4, "col": 8}
    return jax.shard_map(
        per_device if planned else per_device_general,
        mesh=mesh, in_specs=in_specs, out_specs=out_specs, check_vma=False,
    )
```

time: 238 us -> 183 us (0.77)
  waiting for transfers between devices: 204 us -> 0 us
  Pallas kernels: 0 us -> 170 us
  matrix products: 16.8 us -> 0 us
  between operations: 14.1 us -> 0.66 us
  local copies, waits for them, and re-layouts: 2.15 us -> 12.6 us
    all_gather x2 -> x0, waiting for transfers between devices: 203 us -> none  [the longest x1 175 us: per_device(): gathered_w = lax.all_gather(weight, 'row', axis=0, tiled=True)]
    pallas_call x0 -> x1, Pallas kernels: none -> 170 us  [per_device(): pl.pallas_call(functools.partial(kernel, orients, nc, cw), out_shape=jax....]
    dot_general x1 -> x0, matrix products: 16.8 us -> none  [per_device(): product = jnp.dot(aligned, gathered_w, preferred_element_type=jnp.float32)]
    unnamed x2, local copies, waits for them, and re-layouts: 0.01 us -> 12.6 us
  transfers between devices with their start and end apart: 2 -> 0, of which waited for: 2 -> 0; matrix products, arithmetic and copies ran while one was open for 1% -> 0% of each run, Pallas kernels for 0% -> 0%
where the time goes in v1:
time: 183 us
  Pallas kernels  170 us (93%)
  local copies, waits for them, and re-layouts  12.6 us (7%)
    pallas_call x1, Pallas kernels, per_device(): pl.pallas_call(functools.partial(kernel, orients, nc, cw), out_shape=jax....  170 us
    unnamed x2, local copies, waits for them, and re-layouts  12.6 us

profile of v1, /device:TPU:0, one launch (start us, length us, event | category | flops | bytes accessed | tf_op | source)
XLA Modules:
  0.0 183.1 jit_solution(6058725703552896116)
XLA Ops:
  0.7 1.8 copy.5.tok_in
  2.4 169.9 %shard_map.46 = f32[512,6144]{1,0:T(8,128)} custom-call(s32[1]{0:T(128)S(6)} %copy.7.counts, s32[4]{0:T(128)} %owner.1, bf16[512,192]{1,0:T(8,128)(2,1)} %copy.5.tok_in, bf16[384,6144]{1,0:T(8,128)(2,1)} %w_in.1), custom_call_target="tpu_custom_call" | custom-call | flops 9663676416 | bytes 25165824 | tf_op jit(solution)/shard_map/pallas_call | solution.py:213
  172.3 10.8 %copy.8 = f32[512,6144]{1,0:T(8,128)} copy(f32[512,6144]{1,0:T(8,128)} %shard_map.46) | data formatting | bytes 25165824

commit v2 on v1

--- a/solution.py
+++ b/solution.py
@@ -31,8 +31,8 @@
 def kernel(
     orients, nc, cw,
     counts, owner, tok_in, w_in, out,
-    tokb, al, wb, qb, qs, rb, rs, ob,
-    tl_sem, ta_s, ta_r, tb_s, tb_r,
+    piece_buf, tokb, al, wb, qb, qs, rb, rs, ob,
+    tl_sem, tc_s, tc_r, ta_s, ta_r, zr_s, zr_r, zl_s, zl_r, tm_s, tm_r,
     wl_sem, px_s, px_r, py_s, py_r, fy_s, fy_r, ox_s, ox_r, os_s, os_r, ol_sem,
 ):
     rows, piece = tok_in.shape
@@ -41,13 +41,13 @@
     row, col = lax.axis_index("row"), lax.axis_index("col")
     y, x = row // 2, row % 2
     z, core = col // 2, col % 2
-    z_hi, z_lo = z // 2, z % 2
+    part = rows // 2
     x_dev = (y * 2 + (1 - x), col)
     y_dev = ((1 - y) * 2 + x, col)
-    z1_dev = (row, (z_hi * 2 + (1 - z_lo)) * 2 + core)
-    z2_dev = (row, ((1 - z_hi) * 2 + z_lo) * 2 + core)
+    up_dev = (row, lax.rem(z + 1, 4) * 2 + core)
+    down_dev = (row, lax.rem(z + 3, 4) * 2 + core)
     c_dev = (row, z * 2 + (1 - core))
-    peers = (x_dev, y_dev, z1_dev, z2_dev, c_dev)
+    peers = (x_dev, y_dev, up_dev, down_dev, c_dev)
 
     barrier = pltpu.get_barrier_semaphore()
     for peer in peers:
@@ -113,50 +113,116 @@
             return carry
         lax.fori_loop(0, nc, body, 0)
 
-    own = pltpu.make_async_copy(tok_in, tokb.at[core, z, 0], tl_sem)
+    def start_weights(k):
+        for o in orients:
+            px(o, k).start()
+            py(o, k).start()
+
+    def rows_of(c):
+        return pl.ds(pl.multiple_of(c * part, 16), part)
+
+    own = pltpu.make_async_copy(tok_in.at[rows_of(core)], piece_buf.at[0], tl_sem)
     own.start()
-    first = [remote(tok_in, tokb.at[core, z, 1 + i], ta_s.at[i], ta_r.at[i], a_dev[o])
+    other = remote(tok_in.at[rows_of(1 - core)], piece_buf.at[1], tc_s, tc_r, c_dev)
+    other.start()
+    start_weights(0)
+    own.wait()
+    other.wait()
+    mine_t, other_t = piece_buf[0], piece_buf[1]
+
+    @pl.when(core == 0)
+    def _():
+        tokb[0, z, 0] = jnp.concatenate([mine_t, other_t], axis=1)
+
+    @pl.when(core == 1)
+    def _():
+        tokb[1, z, 0] = jnp.concatenate([other_t, mine_t], axis=1)
+
+    first = [remote(tokb.at[core, z, 0], tokb.at[core, z, 1 + i], ta_s.at[i], ta_r.at[i], a_dev[o])
              for i, o in enumerate(orients)]
     for c in first:
         c.start()
-
-    def start_weights(o, k):
-        px(o, k).start()
-        py(o, k).start()
+    start_weights(1)
+    for c in first:
+        c.wait_recv()
+
+    def slot_copy(at_z, send, recv, dev):
+        return remote(tokb.at[core, at_z], tokb.at[core, at_z], send, recv, dev)
+
+    def mate(at_z):
+        return slot_copy(at_z, tm_s.at[at_z], tm_r.at[at_z], c_dev)
+
+    def up(s, shard):
+        return slot_copy(shard, zr_s.at[s], zr_r.at[s], up_dev)
+
+    def down(s, shard):
+        return slot_copy(shard, zl_s.at[s], zl_r.at[s], down_dev)
+
+    def send_step(s):
+        @pl.when(jnp.logical_and(z < 3, z >= s))
+        def _():
+            up(s, z - s).start()
+
+        @pl.when(jnp.logical_and(z > 0, z + s <= 3))
+        def _():
+            down(s, z + s).start()
+
+    def recv_step(s):
+        @pl.when(z >= s + 1)
+        def _():
+            up(s, z - 1 - s).wait_recv()
+            mate(z - 1 - s).start()
+
+        @pl.when(z + 1 + s <= 3)
+        def _():
+            down(s, z + 1 + s).wait_recv()
+            mate(z + 1 + s).start()
+
+    send_step(0)
+    mate(z).start()
+
+    def start_rest(k, carry):
+        start_weights(k)
+        return carry
+    lax.fori_loop(2, nc, start_rest, 0)
+
+    def start_own(o, k):
         wl(o, k).start()
-    each(start_weights)
-
-    own.wait()
+    each(start_own)
+
+    def forward(o, k):
+        px(o, k).wait_recv()
+        fy(o, k).start()
+
+    ahead = 3
+    for s in range(3):
+        recv_step(s)
+        if s < 2:
+            send_step(s + 1)
+        for o in orients:
+            forward(o, s)
+    for s in range(3):
+        @pl.when(jnp.logical_and(z < 3, z >= s))
+        def _():
+            up(s, z - s).wait_send()
+
+        @pl.when(jnp.logical_and(z > 0, z + s <= 3))
+        def _():
+            down(s, z + s).wait_send()
+    for at_z in range(4):
+        mate(at_z).wait_recv()
+        mate(at_z).wait_send()
     for c in first:
-        c.wait()
-    pair = pl.ds(z_hi * 2, 2)
-    steps = (
-        remote(tokb.at[core, z], tokb.at[core, z], tb_s.at[0], tb_r.at[0], z1_dev),
-        remote(tokb.at[core, pair], tokb.at[core, pair], tb_s.at[1], tb_r.at[1], z2_dev),
-        remote(tokb.at[core], tokb.at[core], tb_s.at[2], tb_r.at[2], c_dev),
-    )
-    for c in steps:
-        c.start()
-        c.wait()
+        c.wait_send()
 
     order = (row, y * 2 + (1 - x), (1 - y) * 2 + x, (1 - y) * 2 + (1 - x))
     for j in range(4):
         slot = owner[order[j]]
         for s in range(1 + len(orients)):
-            lo = tokb[0, slot, s]
-            hi = tokb[1, slot, s]
-            al[s, :, j * panel:(j + 1) * panel] = jnp.concatenate([lo, hi], axis=1)
+            for c in range(2):
+                al[s, c * part:(c + 1) * part, j * panel:(j + 1) * panel] = tokb[c, slot, s]
 
     kept = lax.broadcasted_iota(jnp.int32, (rows, cw), 0) < counts[0]
-
-    def forward(o, k):
-        px(o, k).wait_recv()
-        fy(o, k).start()
-
-    ahead = 2
-    for k in range(ahead):
-        for o in orients:
-            forward(o, k)
 
     def compute(o, k):
         g = at(o, k)
@@ -216,7 +282,8 @@
         in_specs=[pl.BlockSpec(memory_space=pltpu.SMEM)] * 2 + [pl.BlockSpec(memory_space=pl.ANY)] * 2,
         out_specs=pl.BlockSpec(memory_space=pl.ANY),
         scratch_shapes=[
-            pltpu.VMEM((2, 4, sets, rows, piece), jnp.bfloat16),
+            pltpu.VMEM((2, rows // 2, piece), jnp.bfloat16),
+            pltpu.VMEM((2, 4, sets, rows // 2, panel), jnp.bfloat16),
             pltpu.VMEM((sets, rows, 4 * panel), jnp.bfloat16),
             pltpu.VMEM((nct, 4, panel, cw), jnp.bfloat16),
             pltpu.VMEM((nct, rows, cw), jnp.int16),
@@ -224,7 +291,8 @@
             pltpu.VMEM((nct, rows, cw), jnp.int16),
             pltpu.VMEM((nct, GROUPS, cw), jnp.float32),
             pltpu.VMEM((2, nct, rows, cw), jnp.float32),
-            dma, dma((len(orients),)), dma((len(orients),)), dma((3,)), dma((3,)),
+            dma, dma, dma, dma((len(orients),)), dma((len(orients),)),
+            dma((3,)), dma((3,)), dma((3,)), dma((3,)), dma((4,)), dma((4,)),
         ] + [dma((nct,))] * 11 + [dma((2, nct))],
         compiler_params=pltpu.CompilerParams(
             collective_id=0, has_side_effects=True, vmem_limit_bytes=56 * 2**20),

time: 183 us -> 139 us (0.76)
  Pallas kernels: 170 us -> 126 us
    pallas_call x1, Pallas kernels: 170 us -> 126 us  [per_device(): pl.pallas_call(functools.partial(kernel, orients, nc, cw), out_shape=jax....]
where the time goes in v2:
time: 139 us
  Pallas kernels  126 us (91%)
  local copies, waits for them, and re-layouts  12.6 us (9%)
    pallas_call x1, Pallas kernels, per_device(): pl.pallas_call(functools.partial(kernel, orients, nc, cw), out_shape=jax....  126 us
    unnamed x2, local copies, waits for them, and re-layouts  12.6 us

profile of v2, /device:TPU:0, one launch (start us, length us, event | category | flops | bytes accessed | tf_op | source)
XLA Modules:
  0.0 138.8 jit_solution(12746456335438298862)
XLA Ops:
  0.7 1.8 %copy.5.tok_in = bf16[512,192]{1,0:T(8,128)(2,1)} copy(bf16[512,192]{0,1:T(8,128)(2,1)} %param.4) | data formatting | bytes 393216 | tf_op args[0]
  2.4 125.5 %shard_map.46 = f32[512,6144]{1,0:T(8,128)} custom-call(s32[1]{0:T(128)S(6)} %copy.7.counts, s32[4]{0:T(128)} %owner.1, bf16[512,192]{1,0:T(8,128)(2,1)} %copy.5.tok_in, bf16[384,6144]{1,0:T(8,128)(2,1)} %w_in.1), custom_call_target="tpu_custom_call" | custom-call | flops 9663676416 | bytes 25165824 | tf_op jit(solution)/shard_map/pallas_call | solution.py:279
  127.9 10.8 %copy.8 = f32[512,6144]{1,0:T(8,128)} copy(f32[512,6144]{1,0:T(8,128)} %shard_map.46) | data formatting | bytes 25165824

commit v3 on v2

--- a/solution.py
+++ b/solution.py
@@ -30,12 +30,12 @@
 
 def kernel(
     orients, nc, cw,
-    counts, owner, tok_in, w_in, out,
-    piece_buf, tokb, al, wb, qb, qs, rb, rs, ob,
+    counts, owner, tok_in, w_in, ob,
+    piece_buf, tokb, al, wb, qb, qs, rb, rs,
     tl_sem, tc_s, tc_r, ta_s, ta_r, zr_s, zr_r, zl_s, zl_r, tm_s, tm_r,
-    wl_sem, px_s, px_r, py_s, py_r, fy_s, fy_r, ox_s, ox_r, os_s, os_r, ol_sem,
+    wl_sem, px_s, px_r, py_s, py_r, fy_s, fy_r, ox_s, ox_r, os_s, os_r,
 ):
-    rows, piece = tok_in.shape
+    piece, rows = tok_in.shape
     panel = w_in.shape[0]
     half = nc * cw
     row, col = lax.axis_index("row"), lax.axis_index("col")
@@ -96,16 +96,6 @@
         g = at(o, k)
         return remote(qs.at[g], rs.at[g], os_s.at[g], os_r.at[g], a_dev[o])
 
-    def out_own(o, k):
-        g = at(o, k)
-        return pltpu.make_async_copy(
-            ob.at[0, g], out.at[:, cols(o, side[o], k)], ol_sem.at[0, g])
-
-    def out_got(o, k):
-        g = at(o, k)
-        return pltpu.make_async_copy(
-            ob.at[1, g], out.at[:, cols(o, 1 - side[o], k)], ol_sem.at[1, g])
-
     def each(f):
         def body(k, carry):
             for o in orients:
@@ -119,11 +109,11 @@
             py(o, k).start()
 
     def rows_of(c):
-        return pl.ds(pl.multiple_of(c * part, 16), part)
-
-    own = pltpu.make_async_copy(tok_in.at[rows_of(core)], piece_buf.at[0], tl_sem)
+        return pl.ds(pl.multiple_of(c * part, 128), part)
+
+    own = pltpu.make_async_copy(tok_in.at[:, rows_of(core)], piece_buf.at[0], tl_sem)
     own.start()
-    other = remote(tok_in.at[rows_of(1 - core)], piece_buf.at[1], tc_s, tc_r, c_dev)
+    other = remote(tok_in.at[:, rows_of(1 - core)], piece_buf.at[1], tc_s, tc_r, c_dev)
     other.start()
     start_weights(0)
     own.wait()
@@ -132,11 +122,11 @@
 
     @pl.when(core == 0)
     def _():
-        tokb[0, z, 0] = jnp.concatenate([mine_t, other_t], axis=1)
+        tokb[0, z, 0] = jnp.concatenate([mine_t, other_t], axis=0).T
 
     @pl.when(core == 1)
     def _():
-        tokb[1, z, 0] = jnp.concatenate([other_t, mine_t], axis=1)
+        tokb[1, z, 0] = jnp.concatenate([other_t, mine_t], axis=0).T
 
     first = [remote(tokb.at[core, z, 0], tokb.at[core, z, 1 + i], ta_s.at[i], ta_r.at[i], a_dev[o])
              for i, o in enumerate(orients)]
@@ -246,7 +236,6 @@
         os_(o, k).start()
         mine = jnp.dot(al[0], w, preferred_element_type=jnp.float32)
         ob[0, g] = jnp.where(kept, mine, 0.0)
-        out_own(o, k).start()
     each(compute)
 
     def receive(o, k):
@@ -256,15 +245,31 @@
         levels = rb[g].astype(jnp.int32).astype(jnp.float32).reshape(GROUPS, rows // GROUPS, cw)
         value = levels * (rs[g] * (1.0 / 32767.0))[:, None, :]
         ob[1, g] = jnp.where(kept, value.reshape(rows, cw), 0.0)
-        out_got(o, k).start()
     each(receive)
 
     def finish(o, k):
         for c in (px(o, k), py(o, k), fy(o, k), ox(o, k), os_(o, k)):
             c.wait_send()
-        out_own(o, k).wait()
-        out_got(o, k).wait()
     each(finish)
+
+
+def store_kernel(orients, nc, cw, ob, out, sem):
+    row = lax.axis_index("row")
+    side = (row % 2, row // 2)
+
+    def each(act):
+        def body(k, carry):
+            for i, o in enumerate(orients):
+                for got in range(2):
+                    s = 1 - side[o] if got else side[o]
+                    start = pl.multiple_of((i * 2 + s) * nc * cw + k * cw, 128)
+                    copy = pltpu.make_async_copy(
+                        ob.at[got, i * nc + k], out.at[:, pl.ds(start, cw)], sem.at[got, i * nc + k])
+                    act(copy)
+            return carry
+        lax.fori_loop(0, nc, body, 0)
+    each(lambda copy: copy.start())
+    each(lambda copy: copy.wait())
 
 
 def per_device(tokens, weight, counts, owner):
@@ -276,13 +281,13 @@
     nct = nc * len(orients)
     sets = 1 + len(orients)
     dma = pltpu.SemaphoreType.DMA
-    return pl.pallas_call(
+    blocks = pl.pallas_call(
         functools.partial(kernel, orients, nc, cw),
-        out_shape=jax.ShapeDtypeStruct((rows, width), jnp.float32),
+        out_shape=pltpu.VMEM((2, nct, rows, cw), jnp.float32),
         in_specs=[pl.BlockSpec(memory_space=pltpu.SMEM)] * 2 + [pl.BlockSpec(memory_space=pl.ANY)] * 2,
-        out_specs=pl.BlockSpec(memory_space=pl.ANY),
+        out_specs=pl.BlockSpec(memory_space=pltpu.VMEM),
         scratch_shapes=[
-            pltpu.VMEM((2, rows // 2, piece), jnp.bfloat16),
+            pltpu.VMEM((2, piece, rows // 2), jnp.bfloat16),
             pltpu.VMEM((2, 4, sets, rows // 2, panel), jnp.bfloat16),
             pltpu.VMEM((sets, rows, 4 * panel), jnp.bfloat16),
             pltpu.VMEM((nct, 4, panel, cw), jnp.bfloat16),
@@ -290,15 +295,22 @@
             pltpu.VMEM((nct, GROUPS, cw), jnp.float32),
             pltpu.VMEM((nct, rows, cw), jnp.int16),
             pltpu.VMEM((nct, GROUPS, cw), jnp.float32),
-            pltpu.VMEM((2, nct, rows, cw), jnp.float32),
             dma, dma, dma, dma((len(orients),)), dma((len(orients),)),
             dma((3,)), dma((3,)), dma((3,)), dma((3,)), dma((4,)), dma((4,)),
-        ] + [dma((nct,))] * 11 + [dma((2, nct))],
+        ] + [dma((nct,))] * 11,
         compiler_params=pltpu.CompilerParams(
-            collective_id=0, has_side_effects=True, vmem_limit_bytes=56 * 2**20),
+            collective_id=0, has_side_effects=True, vmem_limit_bytes=48 * 2**20),
         cost_estimate=pl.CostEstimate(
             flops=2 * rows * 4 * panel * width, bytes_accessed=8 * rows * width, transcendentals=0),
-    )(counts, owner, tokens, weight)
+    )(counts, owner, tokens.T, weight)
+    return pl.pallas_call(
+        functools.partial(store_kernel, orients, nc, cw),
+        out_shape=jax.ShapeDtypeStruct((rows, width), jnp.float32),
+        in_specs=[pl.BlockSpec(memory_space=pltpu.VMEM)],
+        out_specs=pl.BlockSpec(memory_space=pl.ANY),
+        scratch_shapes=[dma((2, nct))],
+        compiler_params=pltpu.CompilerParams(vmem_limit_bytes=16 * 2**20),
+    )(pltpu.with_memory_space_constraint(blocks, pltpu.VMEM))
 
 
 def solution(mesh):

time: 139 us -> 130 us (0.935)
  local copies, waits for them, and re-layouts: 12.6 us -> 0 us
  Pallas kernels: 126 us -> 129 us
    unnamed x2 -> x0, local copies, waits for them, and re-layouts: 12.6 us -> none
    pallas_call x1 -> x2, Pallas kernels: 126 us -> 129 us  [the longest x1 124 us: per_device(): pl.pallas_call(functools.partial(kernel, orients, nc, cw), out_shape=pltp...]
where the time goes in v3:
time: 130 us
  Pallas kernels  129 us (99%)
    pallas_call x1, Pallas kernels, per_device(): pl.pallas_call(functools.partial(kernel, orients, nc, cw), out_shape=pltp...  124 us
    pallas_call x1, Pallas kernels, per_device(): pl.pallas_call(functools.partial(store_kernel, orients, nc, cw), out_shap...  4.76 us

profile of v3, /device:TPU:0, one launch (start us, length us, event | category | flops | bytes accessed | tf_op | source)
XLA Modules:
  0.0 129.8 jit_solution(2338785523361287075)
XLA Ops:
  0.7 124.4 %shard_map.46.ob = f32[2,12,512,256]{3,2,1,0:T(8,128)S(1)} custom-call(s32[1]{0:T(128)S(6)} %copy.5.counts, s32[4]{0:T(128)} %owner.1, bf16[192,512]{1,0:T(8,128)(2,1)} %bitcast.1, bf16[384,6144]{1,0:T(8,128)(2,1)} %w_in.1), custom_call_target="tpu_custom_call" | custom-call | flops 9663676416 | bytes 25165824 | tf_op jit(solution)/shard_map/pallas_call | solution.py:284
  125.0 4.8 %shard_map.47 = f32[512,6144]{1,0:T(8,128)} custom-call(f32[2,12,512,256]{3,2,1,0:T(8,128)S(1)} %shard_map.46.ob), custom_call_target="tpu_custom_call" | custom-call | tf_op jit(solution)/shard_map/pallas_call | solution.py:306

commit v4 on v3

--- a/solution.py
+++ b/solution.py
@@ -8,7 +8,7 @@
 from jax.sharding import PartitionSpec as P
 
 MESH = pl.DeviceIdType.MESH
-GROUPS = 8
+GROUPS = 2
 
 
 def align_panels(gathered, owner):
@@ -235,55 +235,47 @@
         ox(o, k).start()
         os_(o, k).start()
         mine = jnp.dot(al[0], w, preferred_element_type=jnp.float32)
-        ob[0, g] = jnp.where(kept, mine, 0.0)
+        ob[:, cols(o, side[o], k)] = jnp.where(kept, mine, 0.0)
     each(compute)
 
+    def sent(o, k):
+        for c in (px(o, k), py(o, k), fy(o, k)):
+            c.wait_send()
+    each(sent)
+
     def receive(o, k):
         g = at(o, k)
-        ox(o, k).wait_recv()
-        os_(o, k).wait_recv()
+        ox(o, k).wait()
+        os_(o, k).wait()
         levels = rb[g].astype(jnp.int32).astype(jnp.float32).reshape(GROUPS, rows // GROUPS, cw)
         value = levels * (rs[g] * (1.0 / 32767.0))[:, None, :]
-        ob[1, g] = jnp.where(kept, value.reshape(rows, cw), 0.0)
+        ob[:, cols(o, 1 - side[o], k)] = jnp.where(kept, value.reshape(rows, cw), 0.0)
     each(receive)
 
-    def finish(o, k):
-        for c in (px(o, k), py(o, k), fy(o, k), ox(o, k), os_(o, k)):
-            c.wait_send()
-    each(finish)
-
-
-def store_kernel(orients, nc, cw, ob, out, sem):
-    row = lax.axis_index("row")
-    side = (row % 2, row // 2)
-
-    def each(act):
-        def body(k, carry):
-            for i, o in enumerate(orients):
-                for got in range(2):
-                    s = 1 - side[o] if got else side[o]
-                    start = pl.multiple_of((i * 2 + s) * nc * cw + k * cw, 128)
-                    copy = pltpu.make_async_copy(
-                        ob.at[got, i * nc + k], out.at[:, pl.ds(start, cw)], sem.at[got, i * nc + k])
-                    act(copy)
-            return carry
-        lax.fori_loop(0, nc, body, 0)
-    each(lambda copy: copy.start())
-    each(lambda copy: copy.wait())
+
+def store_kernel(parts, ob, out, sem):
+    step = ob.shape[0] // parts
+    copies = [pltpu.make_async_copy(ob.at[pl.ds(i * step, step)], out.at[pl.ds(i * step, step)], sem.at[i])
+              for i in range(parts)]
+    for c in copies:
+        c.start()
+    for c in copies:
+        c.wait()
 
 
 def per_device(tokens, weight, counts, owner):
     rows, piece = tokens.shape
     panel, width = weight.shape
     orients = (0, 1)
-    cw = 256
+    cw = 512
+    parts = 8
     nc = width // (2 * len(orients) * cw)
     nct = nc * len(orients)
     sets = 1 + len(orients)
     dma = pltpu.SemaphoreType.DMA
     blocks = pl.pallas_call(
         functools.partial(kernel, orients, nc, cw),
-        out_shape=pltpu.VMEM((2, nct, rows, cw), jnp.float32),
+        out_shape=pltpu.VMEM((rows, width), jnp.float32),
         in_specs=[pl.BlockSpec(memory_space=pltpu.SMEM)] * 2 + [pl.BlockSpec(memory_space=pl.ANY)] * 2,
         out_specs=pl.BlockSpec(memory_space=pltpu.VMEM),
         scratch_shapes=[
@@ -304,11 +296,11 @@
             flops=2 * rows * 4 * panel * width, bytes_accessed=8 * rows * width, transcendentals=0),
     )(counts, owner, tokens.T, weight)
     return pl.pallas_call(
-        functools.partial(store_kernel, orients, nc, cw),
+        functools.partial(store_kernel, parts),
         out_shape=jax.ShapeDtypeStruct((rows, width), jnp.float32),
         in_specs=[pl.BlockSpec(memory_space=pltpu.VMEM)],
         out_specs=pl.BlockSpec(memory_space=pl.ANY),
-        scratch_shapes=[dma((2, nct))],
+        scratch_shapes=[dma((parts,))],
         compiler_params=pltpu.CompilerParams(vmem_limit_bytes=16 * 2**20),
     )(pltpu.with_memory_space_constraint(blocks, pltpu.VMEM))
 

time: 130 us -> 129 us (level)
    pallas_call x1, Pallas kernels: 124 us -> 123 us  [per_device(): pl.pallas_call(functools.partial(kernel, orients, nc, cw), out_shape=pltp...]
where the time goes in v4:
time: 129 us; the launch traced here: 128 us
  Pallas kernels  128 us (99%)
    pallas_call x1, Pallas kernels, per_device(): pl.pallas_call(functools.partial(kernel, orients, nc, cw), out_shape=pltp...  123 us
    pallas_call x1, Pallas kernels, per_device(): pl.pallas_call(functools.partial(store_kernel, parts), out_shape=jax.Shap...  4.66 us

profile of v4, /device:TPU:0, one launch (start us, length us, event | category | flops | bytes accessed | tf_op | source)
XLA Modules:
  0.0 128.4 jit_solution(8859603011494593086)
XLA Ops:
  0.7 123.0 %shard_map.46.ob = f32[512,6144]{1,0:T(8,128)S(1)} custom-call(s32[1]{0:T(128)S(6)} %copy.5.counts, s32[4]{0:T(128)} %owner.1, bf16[192,512]{1,0:T(8,128)(2,1)} %bitcast.1, bf16[384,6144]{1,0:T(8,128)(2,1)} %w_in.1), custom_call_target="tpu_custom_call" | custom-call | flops 9663676416 | bytes 25165824 | tf_op jit(solution)/shard_map/pallas_call | solution.py:276
  123.7 4.7 %shard_map.47 = f32[512,6144]{1,0:T(8,128)} custom-call(f32[512,6144]{1,0:T(8,128)S(1)} %shard_map.46.ob), custom_call_target="tpu_custom_call" | custom-call | tf_op jit(solution)/shard_map/pallas_call | solution.py:298

commit v5 on v4

--- a/solution.py
+++ b/solution.py
@@ -267,7 +267,7 @@
     rows, piece = tokens.shape
     panel, width = weight.shape
     orients = (0, 1)
-    cw = 512
+    cw = 384
     parts = 8
     nc = width // (2 * len(orients) * cw)
     nct = nc * len(orients)

time: 129 us -> 129 us (level)
  no operation moved by 1% of the time
where the time goes in v5:
time: 129 us; the launch traced here: 128 us
  Pallas kernels  128 us (99%)
    pallas_call x1, Pallas kernels, per_device(): pl.pallas_call(functools.partial(kernel, orients, nc, cw), out_shape=pltp...  123 us
    pallas_call x1, Pallas kernels, per_device(): pl.pallas_call(functools.partial(store_kernel, parts), out_shape=jax.Shap...  4.66 us

profile of v5, /device:TPU:0, one launch (start us, length us, event | category | flops | bytes accessed | tf_op | source)
XLA Modules:
  0.0 128.5 jit_solution(17921017636790352338)
XLA Ops:
  0.7 123.2 %shard_map.46.ob = f32[512,6144]{1,0:T(8,128)S(1)} custom-call(s32[1]{0:T(128)S(6)} %copy.5.counts, s32[4]{0:T(128)} %owner.1, bf16[192,512]{1,0:T(8,128)(2,1)} %bitcast.1, bf16[384,6144]{1,0:T(8,128)(2,1)} %w_in.1), custom_call_target="tpu_custom_call" | custom-call | flops 9663676416 | bytes 25165824 | tf_op jit(solution)/shard_map/pallas_call | solution.py:276
  123.8 4.7 %shard_map.47 = f32[512,6144]{1,0:T(8,128)} custom-call(f32[512,6144]{1,0:T(8,128)S(1)} %shard_map.46.ob), custom_call_target="tpu_custom_call" | custom-call | tf_op jit(solution)/shard_map/pallas_call | solution.py:298
